TPU v7x, 32 devices: a whole 2x2x4 slice. The times are simulated.
32 devices in a mesh: dp: 1, expert: 32 (over z, y, x, core).
Axes of the slice: x: 2, y: 2, z: 4, core: 2. Of those that a mesh axis runs over, the one named last changes fastest.
Arguments:
- queries: bfloat16 [1024, 4096], P('dp', 'expert'), may hold values from -140 to 140
- keys: bfloat16 [1024, 256], P(('dp', 'expert')), may hold values from -4 to 4
- values: bfloat16 [1024, 256], P(('dp', 'expert')), may hold values from -4 to 4
- span_ids: int32 [1024], P('dp'), may hold values from 0 to 9, as said below
- residual: bfloat16 [1024, 4096], P(('dp', 'expert')), may hold values from -6 to 6
- norm_gain: float32 [4096], replicated, may hold values from 0.1 to 1.9
- routes: int32 [1024, 8], P(('dp', 'expert')), may hold values from 0 to 127, as said below
- gates: float32 [1024, 8], P(('dp', 'expert')), may hold values from 0.2 to 1
- w_gate: bfloat16 [4096, 4096], P('expert'), may hold values from -0.09375 to 0.09375
- w_up: bfloat16 [4096, 4096], P('expert'), may hold values from -0.09375 to 0.09375
- w_down: bfloat16 [4096, 4096], P('expert'), may hold values from -0.1875 to 0.1875
Outputs:
- mixed: bfloat16 [1024, 4096], P(('dp', 'expert'))
Inputs may be any that keep to these rules, and one draw needn't show every extreme that they name: `span_ids`: span numbers start at 0 and never fall along the positions; every span starts at an even position, has 2 to 512 positions and never crosses a multiple of 512; one aligned block of 512 positions is a single span, and every other holds exactly 9 spans. `routes`: each row names 8 different experts. In the rows of one device (aligned blocks of 32 rows) each expert below 4 is named by at most 8 rows, and exactly one such expert, changing from block to block, by exactly 8 rows; every expert below 4 is that one in some block.
All inputs are finite; a program needn't handle non-finite values.
Results may differ from a plain program's by a relative error of at most 0.0054.
Values may be sent and summed in bfloat16 or wider, within the bound.
A program may use at most 64 MiB of HBM per device.

v0:
```python
import math
import jax
import jax.numpy as jnp
from jax import lax
from jax.sharding import PartitionSpec as P

KV_HEADS = 4
HEAD_DIM = 64
FF_WIN = 1024
SPAN = 512


def from_partner(value, axis, distance):
    mask = 2**distance
    pairs = [(source, source ^ mask) for source in range(lax.axis_size(axis))]
    return lax.ppermute(value, axis, pairs)


def attend(queries, key_mine, value_mine, span_ids):
    tokens_all, head_width = queries.shape
    heads_here = head_width // HEAD_DIM
    blocks = tokens_all // SPAN
    score_scale = 1.0 / math.sqrt(HEAD_DIM)
    positions = jnp.arange(SPAN)
    causal = positions[None, :] <= positions[:, None]

    def one_block(pieces):
        query_blk, key_blk, value_blk, ids_blk = pieces
        scores = (
            jnp.einsum("qhd,kd->hqk", query_blk, key_blk, preferred_element_type=jnp.float32)
            * score_scale
        )
        allowed = causal & (ids_blk[None, :] == ids_blk[:, None])
        scores = jnp.where(allowed[None], scores, -jnp.inf)
        highest = jnp.max(scores, axis=-1, keepdims=True)
        raised = jnp.exp(scores - highest)
        attn_weights = (raised / jnp.sum(raised, axis=-1, keepdims=True)).astype(jnp.bfloat16)
        attended_blk = jnp.einsum(
            "hqk,kd->qhd", attn_weights, value_blk, preferred_element_type=jnp.float32
        )
        return attended_blk.astype(jnp.bfloat16)

    result = lax.map(
        one_block,
        (
            queries.reshape(blocks, SPAN, heads_here, HEAD_DIM),
            key_mine.reshape(blocks, SPAN, HEAD_DIM),
            value_mine.reshape(blocks, SPAN, HEAD_DIM),
            span_ids.reshape(blocks, SPAN),
        ),
    )
    return result.reshape(tokens_all, head_width)


def shards(
    queries, keys, values, span_ids, residual, norm_gain, routes, gates, w_gate, w_up, w_down
):
    devices = lax.axis_size("expert")
    my_index = lax.axis_index("expert")
    tok_local = residual.shape[0]
    joined = jnp.concatenate(
        [
            keys.reshape(tok_local, KV_HEADS, HEAD_DIM),
            values.reshape(tok_local, KV_HEADS, HEAD_DIM),
        ],
        axis=2,
    )
    spread = jnp.repeat(joined, devices // KV_HEADS, axis=1)
    arrived_heads = lax.all_to_all(spread, "expert", split_axis=1, concat_axis=0, tiled=True)
    key_mine = arrived_heads[:, 0, :HEAD_DIM]
    value_mine = arrived_heads[:, 0, HEAD_DIM:]
    attended_heads = attend(queries, key_mine, value_mine, span_ids)
    attended = lax.all_to_all(attended_heads, "expert", split_axis=0, concat_axis=1, tiled=True)
    stream_wide = residual.astype(jnp.float32) + attended.astype(jnp.float32)
    stream = stream_wide.astype(jnp.bfloat16)
    stream_wide = stream.astype(jnp.float32)
    inverse = lax.rsqrt(jnp.mean(stream_wide * stream_wide, axis=-1, keepdims=True) + 1e-06)
    normed = (stream_wide * inverse * norm_gain).astype(jnp.bfloat16)
    group = FF_WIN // w_gate.shape[0]
    group_bits = group.bit_length() - 1
    wave = devices // group
    capacity = tok_local // 4
    slot_count = capacity // group
    model_width = normed.shape[1]
    expert_ids = jnp.arange(wave, dtype=jnp.int32)
    hits = routes[:, :, None] == expert_ids[None, None, :]
    named = jnp.any(hits, axis=1)
    weight = jnp.sum(jnp.where(hits, gates[:, :, None], 0.0), axis=1)
    slot_index = jnp.cumsum(named.astype(jnp.int32), axis=0) - 1
    selector = named.T[:, None, :] & (
        slot_index.T[:, None, :] == jnp.arange(capacity)[None, :, None]
    )
    outgoing = jnp.einsum(
        "ect,td->ecd", selector.astype(jnp.bfloat16), normed, preferred_element_type=jnp.float32
    ).astype(jnp.bfloat16)
    outgoing = outgoing.reshape(devices, slot_count, model_width)
    gathered = lax.all_to_all(outgoing, "expert", split_axis=0, concat_axis=0, tiled=True)
    for bit_number in range(group_bits):
        partner = from_partner(gathered, "expert", bit_number)
        lower = my_index // 2**bit_number % 2 == 0
        gathered = jnp.where(
            lower,
            jnp.concatenate([gathered, partner], axis=1),
            jnp.concatenate([partner, gathered], axis=1),
        )
    token_rows = gathered.reshape(devices * capacity, model_width)
    dims = (((1,), (1,)), ((), ()))
    gate_pre = lax.dot_general(token_rows, w_gate, dims, preferred_element_type=jnp.float32)
    up_pre = lax.dot_general(token_rows, w_up, dims, preferred_element_type=jnp.float32)
    hidden = (jax.nn.silu(gate_pre) * up_pre).astype(jnp.bfloat16)
    piece = jnp.dot(hidden, w_down, preferred_element_type=jnp.float32).astype(jnp.bfloat16)
    piece = piece.reshape(devices, capacity, model_width)
    returned = lax.all_to_all(piece, "expert", split_axis=0, concat_axis=0, tiled=True)
    expert_out = jnp.sum(
        returned.reshape(wave, group, capacity, model_width).astype(jnp.float32), axis=1
    )
    flat_slots = expert_ids[None, :] * capacity + jnp.maximum(slot_index, 0)
    picked = jnp.take(
        expert_out.reshape(wave * capacity, model_width), flat_slots.reshape(-1), axis=0
    )
    picked = picked.reshape(tok_local, wave, model_width)
    combined = jnp.sum(weight[:, :, None] * picked, axis=1)
    return (stream_wide + combined).astype(jnp.bfloat16)


def solution(mesh):
    return jax.shard_map(
        shards,
        mesh=mesh,
        in_specs=(
            P("dp", "expert"),
            P(("dp", "expert"), None),
            P(("dp", "expert"), None),
            P("dp"),
            P(("dp", "expert"), None),
            P(),
            P(("dp", "expert"), None),
            P(("dp", "expert"), None),
            P("expert", None),
            P("expert", None),
            P("expert", None),
        ),
        out_specs=P(("dp", "expert"), None),
        check_vma=False,
    )
```

profile of v0, /device:TPU:0, one launch (start us, length us, event | category | flops | bytes accessed | tf_op | source)
XLA Modules:
  0.0 171.7 jit_solution(3322995648816507542)
XLA Ops:
  0.0 0.9 reshape.148
  0.9 0.8 reshape.149
  1.8 0.7 broadcast_in_dim.62
  2.6 7.3 %all-to-all-start = ((bf16[32,32,128]{2,0,1:T(8,128)(2,1)}), bf16[32,32,128]{2,0,1:T(8,128)(2,1)S(1)}, u32[]{:S(2)}, u32[]{:S(2)}) async-start(bf16[32,32,128]{2,0,1:T(8,128)(2,1)} %bitcast), calls=%async_computation | async-start | bytes 524288 | tf_op jit(solution)/shard_map/all_to_all | solution.py:69
  9.9 1.2 reshape.169
  11.5 9.0 %all-to-all-done = bf16[32,32,128]{2,0,1:T(8,128)(2,1)S(1)} async-done(((bf16[32,32,128]{2,0,1:T(8,128)(2,1)}), bf16[32,32,128]{2,0,1:T(8,128)(2,1)S(1)}, u32[]{:S(2)}, u32[]{:S(2)}) %all-to-all-start) | async-done | bytes 262176 | tf_op jit(solution)/shard_map/all_to_all | solution.py:69
  20.9 4.6 %while.11 = (s32[]{:T(128)}, bf16[2,512,2,64]{1,3,2,0:T(8,128)(2,1)S(1)}, bf16[2,512,64]{1,2,0:T(8,128)(2,1)S(1)}, s32[2,512]{1,0:T(2,128)S(1)}, bf16[2,512,64]{...) while((s32[]{:T(128)}, bf16[2,512,2,64]{1,3,2,0:T(8,128)(2,1)S(1)}, ...), condition=%wide.region_3.4_spmd.clone, body=%wide.region_0.3_spmd.clone.sunk | while | flops 206899200 | bytes 1393745 | solution.py:43
  21.1 0.9 fusion.104
  22.1 1.1 fusion.105
  23.5 0.9 fusion.104
  24.4 1.1 fusion.105
  26.0 1.0 all_to_all.33
  27.0 2.6 %all-to-all-start.1 = ((bf16[32,32,128]{2,1,0:T(8,128)(2,1)}), bf16[32,32,128]{2,1,0:T(8,128)(2,1)S(1)}, u32[]{:S(2)}, u32[]{:S(2)}) async-start(bf16[32,32,128]{2,1,0:T(8,128)(2,1)} %all_to_all.33), calls=%async_computation.1 | async-start | bytes 524288 | tf_op jit(solution)/shard_map/all_to_all | solution.py:73
  29.8 10.3 %all-to-all-done.1 = bf16[32,32,128]{2,1,0:T(8,128)(2,1)S(1)} async-done(((bf16[32,32,128]{2,1,0:T(8,128)(2,1)}), bf16[32,32,128]{2,1,0:T(8,128)(2,1)S(1)}, u32[]{:S(2)}, u32[]{:S(2)}) %all-to-all-start.1) | async-done | bytes 262176 | tf_op jit(solution)/shard_map/all_to_all | solution.py:73
  41.2 0.8 reduce
  42.2 12.7 %all_to_all.41 = bf16[32,2,2048]{2,1,0:T(2,128)(2,1)S(1)} all-to-all(bf16[32,2,2048]{2,1,0:T(2,128)(2,1)S(1)} %reshape.170), channel_id=1, replica_groups=mesh['dp'=1,'expert'=32] {'expert'}, dimensions={0} | all-to-all | bytes 524288 | tf_op jit(solution)/shard_map/all_to_all | solution.py:97
  55.2 1.9 %collective-permute-done = bf16[32,1,4096]{2,1,0:T(2,128)(2,1)S(1)} collective-permute-done((bf16[32,1,4096]{2,1,0:T(2,128)(2,1)S(1)}, bf16[32,1,4096]{2,1,0:T(2,128)(2,1)S(1)}, u32[]{:S(2)}, u32[]{:S(2)}) %collective-permute-start) | collective-permute-done | bytes 262176 | tf_op jit(solution)/shard_map/ppermute | solution.py:16
  57.1 2.3 %broadcast_select_fusion = bf16[32,2,4096]{2,1,0:T(2,128)(2,1)S(1)} fusion(pred[]{:T(512)S(6)} %eq.61, bf16[32,1,4096]{2,1,0:T(2,128)(2,1)S(1)} %collective-permute-done, bf16[32,1,4096]{2,1,0:T(2,128)(2,1)S(1)} %reshape.171), kind=kLoop, calls=%fused_computation.44 | loop fusion | flops 2359296 | bytes 1048577 | tf_op jit(solution)/shard_map/jit(_where)/select_n | solution.py:101
  59.5 0.5 collective-permute-start.1
  60.0 13.5 %collective-permute-done.1 = bf16[32,2,4096]{2,1,0:T(2,128)(2,1)S(1)} collective-permute-done((bf16[32,2,4096]{2,1,0:T(2,128)(2,1)S(1)}, bf16[32,2,4096]{2,1,0:T(2,128)(2,1)S(1)}, u32[]{:S(2)}, u32[]{:S(2)}) %collective-permute-start.1) | collective-permute-done | bytes 524320 | tf_op jit(solution)/shard_map/ppermute | solution.py:16
  73.5 1.9 %maximum_select_fusion.1 = bf16[32,4,4096]{2,1,0:T(4,128)(2,1)S(1)} fusion(bf16[32,2,4096]{2,1,0:T(2,128)(2,1)S(1)} %collective-permute-done.1, bf16[32,2,4096]{2,1,0:T(2,128)(2,1)S(1)} %broadcast_select_fusion, pred[]{:T(512)S(6)} %eq.60), kind=kLoop, calls=%fused_computation.43 | loop fusion | flops 4718592 | bytes 2097153 | tf_op jit(solution)/shard_map/jit(_where)/select_n | solution.py:101
  75.4 1.0 collective-permute-start.2
  76.3 23.6 %collective-permute-done.2 = bf16[32,4,4096]{2,1,0:T(4,128)(2,1)} collective-permute-done((bf16[32,4,4096]{2,1,0:T(4,128)(2,1)S(1)}, bf16[32,4,4096]{2,1,0:T(4,128)(2,1)}, u32[]{:S(2)}, u32[]{:S(2)}) %collective-permute-start.2) | collective-permute-done | bytes 1048608 | tf_op jit(solution)/shard_map/ppermute | solution.py:16
  99.9 4.0 %fusion.57 = f32[256,128]{1,0:T(8,128)S(1)} fusion(bf16[128,4096]{1,0:T(8,128)(2,1)} %param.22, bf16[32,4,4096]{2,1,0:T(4,128)(2,1)} %collective-permute-done.2, bf16[32,4,4096]{2,1,0:T(4,128)(2,1)S(1)} %maximum_select_fusion.1, pred[]{:T(512)S(6)} %eq.59), kind=kOutput, calls=%fused_computation.55 | convolution fusion | flops 277872640 | bytes 3276801 | tf_op jit(solution)/shard_map/dot_general | solution.py:109
  103.9 6.2 %fusion.49 = bf16[32,8,4096]{2,1,0:T(8,128)(2,1)} fusion(bf16[128,4096]{1,0:T(8,128)(2,1)S(1)} %copy-done, f32[256,128]{1,0:T(8,128)S(1)} %fusion.57, bf16[128,4096]{1,0:T(8,128)(2,1)S(1)} %copy-done.6, bf16[32,4,4096]{2,1,0:T(4,128)(2,1)} %collective-permute-done.2, bf16[32,4,4096]{2,1,0:T(4,128)(2,1)S(1)} %maximum_select_fusion.1, pred[]{:T(512)S(6)} %eq.59), kind=kOutput, calls=%fused_computation.36 | convolution fusion | flops 547553280 | bytes 6422529 | tf_op jit(solution)/shard_map/dot_general | solution.py:111
  110.1 3.8 %all-to-all-start.3 = ((bf16[32,8,4096]{2,1,0:T(8,128)(2,1)}), bf16[32,8,4096]{2,1,0:T(8,128)(2,1)}, u32[]{:S(2)}, u32[]{:S(2)}) async-start(bf16[32,8,4096]{2,1,0:T(8,128)(2,1)} %fusion.49), calls=%async_computation.3 | async-start | bytes 4194304 | tf_op jit(solution)/shard_map/all_to_all | solution.py:113
  114.5 48.4 %all-to-all-done.3 = bf16[32,8,4096]{2,1,0:T(8,128)(2,1)} async-done(((bf16[32,8,4096]{2,1,0:T(8,128)(2,1)}), bf16[32,8,4096]{2,1,0:T(8,128)(2,1)}, u32[]{:S(2)}, u32[]{:S(2)}) %all-to-all-start.3) | async-done | bytes 2097184 | tf_op jit(solution)/shard_map/all_to_all | solution.py:113
  162.9 2.0 %convert_reduce_fusion = f32[4,8,4096]{2,1,0:T(8,128)S(1)} fusion(bf16[32,8,4096]{2,1,0:T(8,128)(2,1)} %all-to-all-done.3), kind=kLoop, calls=%fused_computation.39 | loop fusion | flops 1966080 | bytes 2621440 | tf_op jit(solution)/shard_map/reduce_sum | solution.py:114
  164.8 2.6 %gather_fusion = f32[128,4096]{1,0:T(8,128)} fusion(f32[32,4096]{1,0:T(8,128)S(1)} %bitcast.111, s32[1024]{0:T(1024)S(1)} %pad_clamp_fusion), kind=kCustom, calls=%fused_computation | custom fusion | bytes 4194816 | tf_op jit(solution)/shard_map/jit(_take)/gather | solution.py:118
  167.4 1.9 %gather.7 = f32[32,4,4096]{2,1,0:T(4,128)S(1)} reshape(f32[128,4096]{1,0:T(8,128)} %gather_fusion) | data formatting | bytes 4194304 | tf_op jit(solution)/shard_map/jit(_take)/gather | solution.py:118
  169.3 1.7 multiply_reduce_fusion
  170.9 0.8 fusion.55
  (49 shorter events, 4.1 us)
Async XLA Ops:
  0.0 103.9 %copy-start = (bf16[128,4096]{1,0:T(8,128)(2,1)S(1)}, bf16[128,4096]{1,0:T(8,128)(2,1)}, u32[]{:S(2)}) copy-start(bf16[128,4096]{1,0:T(8,128)(2,1)} %param.23) | copy-start | bytes 3145732
  0.0 11.5 %copy-start.4 = (s32[1024]{0:T(1024)S(1)}, s32[1024]{0:T(1024)}, u32[]{:S(2)}) copy-start(s32[1024]{0:T(1024)} %param.16) | copy-start | bytes 12292
  2.6 17.9 %all-to-all-start = ((bf16[32,32,128]{2,0,1:T(8,128)(2,1)}), bf16[32,32,128]{2,0,1:T(8,128)(2,1)S(1)}, u32[]{:S(2)}, u32[]{:S(2)}) async-start(bf16[32,32,128]{2,0,1:T(8,128)(2,1)} %bitcast), calls=%async_computation | async-start | bytes 524288 | tf_op jit(solution)/shard_map/all_to_all | solution.py:69
  25.5 4.0 %copy-start.3 = (s32[32,8]{0,1:T(8,128)S(1)}, s32[32,8]{0,1:T(8,128)}, u32[]{:S(2)}) copy-start(s32[32,8]{0,1:T(8,128)} %param.19) | copy-start | bytes 3076
  25.6 14.6 %copy-start.1 = (bf16[32,4096]{1,0:T(8,128)(2,1)S(1)}, bf16[32,4096]{1,0:T(8,128)(2,1)}, u32[]{:S(2)}) copy-start(bf16[32,4096]{1,0:T(8,128)(2,1)} %param.17) | copy-start | bytes 786436
  25.6 14.8 %copy-start.2 = (f32[4096]{0:T(1024)S(1)}, f32[4096]{0:T(1024)}, u32[]{:S(2)}) copy-start(f32[4096]{0:T(1024)} %param.18) | copy-start | bytes 49156
  27.0 13.2 %all-to-all-start.1 = ((bf16[32,32,128]{2,1,0:T(8,128)(2,1)}), bf16[32,32,128]{2,1,0:T(8,128)(2,1)S(1)}, u32[]{:S(2)}, u32[]{:S(2)}) async-start(bf16[32,32,128]{2,1,0:T(8,128)(2,1)} %all_to_all.33), calls=%async_computation.1 | async-start | bytes 524288 | tf_op jit(solution)/shard_map/all_to_all | solution.py:73
  55.1 2.0 %collective-permute-start = (bf16[32,1,4096]{2,1,0:T(2,128)(2,1)S(1)}, bf16[32,1,4096]{2,1,0:T(2,128)(2,1)S(1)}, u32[]{:S(2)}, u32[]{:S(2)}) collective-permute-start(bf16[32,1,4096]{2,1,0:T(2,128)(2,1)S(1)} %reshape.171), channel_id=1, source_target_pairs={{0,1},{1,0},{2,3},{3,2},{4,5},{5,4},{6,7},{7,6},{8,9},{9,8},{10,11... | collective-permute-start | bytes 786440 | tf_op jit(solution)/shard_map/ppermute | solution.py:16
  59.5 14.0 %collective-permute-start.1 = (bf16[32,2,4096]{2,1,0:T(2,128)(2,1)S(1)}, bf16[32,2,4096]{2,1,0:T(2,128)(2,1)S(1)}, u32[]{:S(2)}, u32[]{:S(2)}) collective-permute-start(bf16[32,2,4096]{2,1,0:T(2,128)(2,1)S(1)} %broadcast_select_fusion), channel_id=1, source_target_pairs={{0,2},{1,3},{2,0},{3,1},{4,6},{5,7},{6,4},{7,5},{8,10},{9,11},{10,... | collective-permute-start | bytes 1572872 | tf_op jit(solution)/shard_map/ppermute | solution.py:16
  75.4 24.5 %collective-permute-start.2 = (bf16[32,4,4096]{2,1,0:T(4,128)(2,1)S(1)}, bf16[32,4,4096]{2,1,0:T(4,128)(2,1)}, u32[]{:S(2)}, u32[]{:S(2)}) collective-permute-start(bf16[32,4,4096]{2,1,0:T(4,128)(2,1)S(1)} %maximum_select_fusion.1), channel_id=1, source_target_pairs={{0,4},{1,5},{2,6},{3,7},{4,0},{5,1},{6,2},{7,3},{8,12},{9,13},{10,... | collective-permute-start | bytes 3145736 | tf_op jit(solution)/shard_map/ppermute | solution.py:16
  76.3 27.6 %copy-start.6 = (bf16[128,4096]{1,0:T(8,128)(2,1)S(1)}, bf16[128,4096]{1,0:T(8,128)(2,1)}, u32[]{:S(2)}) copy-start(bf16[128,4096]{1,0:T(8,128)(2,1)} %param.21) | copy-start | bytes 3145732
  110.1 4.2 %copy-start.5 = (f32[32,8]{0,1:T(8,128)S(1)}, f32[32,8]{0,1:T(8,128)}, u32[]{:S(2)}) copy-start(f32[32,8]{0,1:T(8,128)} %param.20) | copy-start | bytes 3076
  110.1 52.7 %all-to-all-start.3 = ((bf16[32,8,4096]{2,1,0:T(8,128)(2,1)}), bf16[32,8,4096]{2,1,0:T(8,128)(2,1)}, u32[]{:S(2)}, u32[]{:S(2)}) async-start(bf16[32,8,4096]{2,1,0:T(8,128)(2,1)} %fusion.49), calls=%async_computation.3 | async-start | bytes 4194304 | tf_op jit(solution)/shard_map/all_to_all | solution.py:113
where the time goes:
time: 172 us
  waiting for transfers between devices  107 us (62%)
  starting transfers between devices  15.3 us (9%)
  matrix products  14.6 us (8%)
  blocking collectives  12.7 us (7%)
  local copies, waits for them, and re-layouts  11.8 us (7%)
  other arithmetic  10.4 us (6%)
    all_to_all x1, waiting for transfers between devices, shards(): lax.all_to_all(piece, 'expert', split_axis=0, concat_axis=0, tiled=True)  48.4 us
    ppermute x3, waiting for transfers between devices, from_partner(): return lax.ppermute(value, axis, pairs)  39 us
    all_to_all x1, blocking collectives, shards(): lax.all_to_all(outgoing, 'expert', split_axis=0, concat_axis=0, tiled=True)  12.7 us
    all_to_all x1, waiting for transfers between devices, shards(): lax.all_to_all(attended_heads, 'expert', split_axis=0, concat_axis=1, til...  10.3 us
    all_to_all x1, waiting for transfers between devices, shards(): lax.all_to_all(spread, 'expert', split_axis=1, concat_axis=0, tiled=True)  8.96 us
    all_to_all x1, starting transfers between devices, shards(): lax.all_to_all(spread, 'expert', split_axis=1, concat_axis=0, tiled=True)  7.3 us
    dot_general x1, matrix products, shards(): jnp.dot(hidden, w_down, preferred_element_type=jnp.float32)  6.19 us
    gather x2, local copies, waits for them, and re-layouts, shards(): jnp.take(expert_out.reshape(wave * capacity, model_width), flat_slots.res...  4.43 us
  transfers between devices with their start and end apart: 6, of which 6 were waited for; matrix products, arithmetic and copies ran while one was open for 1% of the time, Pallas kernels for 0%

commit v1 on v0

--- a/solution.py
+++ b/solution.py
@@ -3,6 +3,7 @@
 import jax.numpy as jnp
 from jax import lax
 from jax.sharding import PartitionSpec as P
+from jax.lax import all_to_all, axis_size
 
 KV_HEADS = 4
 HEAD_DIM = 64
@@ -55,6 +56,14 @@
 def shards(
     queries, keys, values, span_ids, residual, norm_gain, routes, gates, w_gate, w_up, w_down
 ):
+
+    def _refer_halves(chunk):
+        b_next = axis_size("expert")
+        before = jnp.split(chunk, b_next, axis=0)
+        ready = jnp.stack(before)
+        r2 = all_to_all(ready, "expert", 0, 0)
+        return jnp.concatenate(r2, axis=1)
+
     devices = lax.axis_size("expert")
     my_index = lax.axis_index("expert")
     tok_local = residual.shape[0]
@@ -70,7 +79,7 @@
     key_mine = arrived_heads[:, 0, :HEAD_DIM]
     value_mine = arrived_heads[:, 0, HEAD_DIM:]
     attended_heads = attend(queries, key_mine, value_mine, span_ids)
-    attended = lax.all_to_all(attended_heads, "expert", split_axis=0, concat_axis=1, tiled=True)
+    attended = _refer_halves(attended_heads)
     stream_wide = residual.astype(jnp.float32) + attended.astype(jnp.float32)
     stream = stream_wide.astype(jnp.bfloat16)
     stream_wide = stream.astype(jnp.float32)

time: 172 us -> 194 us (1.13)
  local copies, waits for them, and re-layouts: 11.8 us -> 33.2 us
    unnamed x19 -> x49, local copies, waits for them, and re-layouts: 1.13 us -> 19.8 us
    another operation x0 -> x33, local copies, waits for them, and re-layouts: none -> 3.51 us  [_refer_halves(): ready = jnp.stack(before)]
where the time goes in v1:
time: 194 us; the launch traced here: 193 us
  waiting for transfers between devices  107 us (55%)
  local copies, waits for them, and re-layouts  33.2 us (17%)
  starting transfers between devices  15.3 us (8%)
  matrix products  14.8 us (8%)
  blocking collectives  12.7 us (7%)
  other arithmetic  10.3 us (5%)
    all_to_all x1, waiting for transfers between devices, shards(): lax.all_to_all(piece, 'expert', split_axis=0, concat_axis=0, tiled=True)  48.4 us
    ppermute x3, waiting for transfers between devices, from_partner(): return lax.ppermute(value, axis, pairs)  39 us
    unnamed x49, local copies, waits for them, and re-layouts  19.8 us
    all_to_all x1, blocking collectives, shards(): lax.all_to_all(outgoing, 'expert', split_axis=0, concat_axis=0, tiled=True)  12.7 us
    all_to_all x1, waiting for transfers between devices, _refer_halves(): r2 = all_to_all(ready, 'expert', 0, 0)  10.3 us
    all_to_all x1, waiting for transfers between devices, shards(): lax.all_to_all(spread, 'expert', split_axis=1, concat_axis=0, tiled=True)  8.97 us
    all_to_all x1, starting transfers between devices, shards(): lax.all_to_all(spread, 'expert', split_axis=1, concat_axis=0, tiled=True)  7.3 us
    dot_general x1, matrix products, shards(): jnp.dot(hidden, w_down, preferred_element_type=jnp.float32)  6.5 us
  transfers between devices with their start and end apart: 6, of which 6 were waited for; matrix products, arithmetic and copies ran while one was open for 1% of the time, Pallas kernels for 0%

profile of v1, /device:TPU:0, one launch (start us, length us, event | category | flops | bytes accessed | tf_op | source)
XLA Modules:
  0.0 193.3 jit_solution(11634511843339990276)
XLA Ops:
  0.0 0.9 reshape.148
  0.9 0.8 reshape.149
  1.8 0.7 broadcast_in_dim.62
  2.6 7.3 %all-to-all-start = ((bf16[32,32,128]{2,0,1:T(8,128)(2,1)}), bf16[32,32,128]{2,0,1:T(8,128)(2,1)S(1)}, u32[]{:S(2)}, u32[]{:S(2)}) async-start(bf16[32,32,128]{2,0,1:T(8,128)(2,1)} %bitcast), calls=%async_computation | async-start | bytes 524288 | tf_op jit(solution)/shard_map/all_to_all | solution.py:78
  9.9 1.2 reshape.170
  11.5 9.0 %all-to-all-done = bf16[32,32,128]{2,0,1:T(8,128)(2,1)S(1)} async-done(((bf16[32,32,128]{2,0,1:T(8,128)(2,1)}), bf16[32,32,128]{2,0,1:T(8,128)(2,1)S(1)}, u32[]{:S(2)}, u32[]{:S(2)}) %all-to-all-start) | async-done | bytes 262176 | tf_op jit(solution)/shard_map/all_to_all | solution.py:78
  20.9 4.6 %while.11 = (s32[]{:T(128)}, bf16[2,512,2,64]{1,3,2,0:T(8,128)(2,1)S(1)}, bf16[2,512,64]{1,2,0:T(8,128)(2,1)S(1)}, s32[2,512]{1,0:T(2,128)S(1)}, bf16[2,512,64]{...) while((s32[]{:T(128)}, bf16[2,512,2,64]{1,3,2,0:T(8,128)(2,1)S(1)}, ...), condition=%wide.region_3.4_spmd.clone, body=%wide.region_0.3_spmd.clone.sunk | while | flops 206899200 | bytes 1393745 | solution.py:44
  21.1 0.9 fusion.105
  22.1 1.1 fusion.106
  23.4 0.9 fusion.105
  24.4 1.1 fusion.106
  26.3 0.6 constant_dynamic-update-slice_fusion.31
  29.7 0.6 constant_dynamic-update-slice_fusion.30
  48.3 2.6 %all-to-all-start.1 = ((bf16[32,32,128]{2,1,0:T(8,128)(2,1)}), bf16[32,32,128]{2,1,0:T(8,128)(2,1)S(1)}, u32[]{:S(2)}, u32[]{:S(2)}) async-start(bf16[32,32,128]{2,1,0:T(8,128)(2,1)} %constant_dynamic-update-slice_fusion), calls=%async_computation.1 | async-start | bytes 524288 | tf_op jit(solution)/shard_map/all_to_all | solution.py:64
  51.2 10.3 %all-to-all-done.1 = bf16[32,32,128]{2,1,0:T(8,128)(2,1)S(1)} async-done(((bf16[32,32,128]{2,1,0:T(8,128)(2,1)}), bf16[32,32,128]{2,1,0:T(8,128)(2,1)S(1)}, u32[]{:S(2)}, u32[]{:S(2)}) %all-to-all-start.1) | async-done | bytes 262176 | tf_op jit(solution)/shard_map/all_to_all | solution.py:64
  62.6 0.8 reduce
  63.5 12.7 %all_to_all.33 = bf16[32,2,2048]{2,1,0:T(2,128)(2,1)S(1)} all-to-all(bf16[32,2,2048]{2,1,0:T(2,128)(2,1)S(1)} %reshape.171), channel_id=1, replica_groups=mesh['dp'=1,'expert'=32] {'expert'}, dimensions={0} | all-to-all | bytes 524288 | tf_op jit(solution)/shard_map/all_to_all | solution.py:106
  76.6 1.9 collective-permute-done
  78.5 2.3 %broadcast_select_fusion = bf16[32,2,4096]{2,1,0:T(2,128)(2,1)S(1)} fusion(pred[]{:T(512)S(6)} %eq.61, bf16[32,1,4096]{2,1,0:T(2,128)(2,1)S(1)} %collective-permute-done, bf16[32,1,4096]{2,1,0:T(2,128)(2,1)S(1)} %reshape.172), kind=kLoop, calls=%fused_computation.44 | loop fusion | flops 2359296 | bytes 1048577 | tf_op jit(solution)/shard_map/jit(_where)/select_n | solution.py:110
  81.4 13.5 %collective-permute-done.1 = bf16[32,2,4096]{2,1,0:T(2,128)(2,1)S(1)} collective-permute-done((bf16[32,2,4096]{2,1,0:T(2,128)(2,1)S(1)}, bf16[32,2,4096]{2,1,0:T(2,128)(2,1)S(1)}, u32[]{:S(2)}, u32[]{:S(2)}) %collective-permute-start.1) | collective-permute-done | bytes 524320 | tf_op jit(solution)/shard_map/ppermute | solution.py:17
  94.9 1.9 maximum_select_fusion.1
  96.8 1.0 collective-permute-start.2
  97.7 23.6 %collective-permute-done.2 = bf16[32,4,4096]{2,1,0:T(4,128)(2,1)} collective-permute-done((bf16[32,4,4096]{2,1,0:T(4,128)(2,1)S(1)}, bf16[32,4,4096]{2,1,0:T(4,128)(2,1)}, u32[]{:S(2)}, u32[]{:S(2)}) %collective-permute-start.2) | collective-permute-done | bytes 1048608 | tf_op jit(solution)/shard_map/ppermute | solution.py:17
  121.3 4.0 %fusion.57 = f32[256,128]{1,0:T(8,128)S(1)} fusion(bf16[128,4096]{1,0:T(8,128)(2,1)} %param.22, bf16[32,4,4096]{2,1,0:T(4,128)(2,1)} %collective-permute-done.2, bf16[32,4,4096]{2,1,0:T(4,128)(2,1)S(1)} %maximum_select_fusion.1, pred[]{:T(512)S(6)} %eq.59), kind=kOutput, calls=%fused_computation.55 | convolution fusion | flops 277872640 | bytes 3276801 | tf_op jit(solution)/shard_map/dot_general | solution.py:118
  125.3 6.5 %fusion.49 = bf16[32,8,4096]{2,1,0:T(8,128)(2,1)} fusion(bf16[128,4096]{1,0:T(8,128)(2,1)S(1)} %copy-done, f32[256,128]{1,0:T(8,128)S(1)} %fusion.57, bf16[128,4096]{1,0:T(8,128)(2,1)} %param.21, bf16[32,4,4096]{2,1,0:T(4,128)(2,1)} %collective-permute-done.2, bf16[32,4,4096]{2,1,0:T(4,128)(2,1)S(1)} %maximum_select_fusion.1, pred[]{:T(512)S(6)} %eq.59), kind=kOutput, calls=%fused_computation.36 | convolution fusion | flops 547553280 | bytes 6422529 | tf_op jit(solution)/shard_map/dot_general | solution.py:120
  131.8 3.8 %all-to-all-start.3 = ((bf16[32,8,4096]{2,1,0:T(8,128)(2,1)}), bf16[32,8,4096]{2,1,0:T(8,128)(2,1)}, u32[]{:S(2)}, u32[]{:S(2)}) async-start(bf16[32,8,4096]{2,1,0:T(8,128)(2,1)} %fusion.49), calls=%async_computation.3 | async-start | bytes 4194304 | tf_op jit(solution)/shard_map/all_to_all | solution.py:122
  136.2 48.4 %all-to-all-done.3 = bf16[32,8,4096]{2,1,0:T(8,128)(2,1)} async-done(((bf16[32,8,4096]{2,1,0:T(8,128)(2,1)}), bf16[32,8,4096]{2,1,0:T(8,128)(2,1)}, u32[]{:S(2)}, u32[]{:S(2)}) %all-to-all-start.3) | async-done | bytes 2097184 | tf_op jit(solution)/shard_map/all_to_all | solution.py:122
  184.5 1.9 %convert_reduce_fusion = f32[4,8,4096]{2,1,0:T(8,128)S(1)} fusion(bf16[32,8,4096]{2,1,0:T(8,128)(2,1)} %all-to-all-done.3), kind=kLoop, calls=%fused_computation.39 | loop fusion | flops 1966080 | bytes 2621440 | tf_op jit(solution)/shard_map/reduce_sum | solution.py:123
  186.5 2.6 %gather_fusion = f32[128,4096]{1,0:T(8,128)} fusion(f32[32,4096]{1,0:T(8,128)S(1)} %bitcast.180, s32[1024]{0:T(1024)S(1)} %pad_clamp_fusion), kind=kCustom, calls=%fused_computation | custom fusion | bytes 4194816 | tf_op jit(solution)/shard_map/jit(_take)/gather | solution.py:127
  189.1 1.9 gather.7
  190.9 1.7 multiply_reduce_fusion
  192.6 0.8 fusion.55
  (113 shorter events, 25.6 us)
Async XLA Ops:
  0.0 125.3 %copy-start = (bf16[128,4096]{1,0:T(8,128)(2,1)S(1)}, bf16[128,4096]{1,0:T(8,128)(2,1)}, u32[]{:S(2)}) copy-start(bf16[128,4096]{1,0:T(8,128)(2,1)} %param.23) | copy-start | bytes 3145732
  0.0 11.5 %copy-start.4 = (s32[1024]{0:T(1024)S(1)}, s32[1024]{0:T(1024)}, u32[]{:S(2)}) copy-start(s32[1024]{0:T(1024)} %param.16) | copy-start | bytes 12292
  2.6 17.9 %all-to-all-start = ((bf16[32,32,128]{2,0,1:T(8,128)(2,1)}), bf16[32,32,128]{2,0,1:T(8,128)(2,1)S(1)}, u32[]{:S(2)}, u32[]{:S(2)}) async-start(bf16[32,32,128]{2,0,1:T(8,128)(2,1)} %bitcast), calls=%async_computation | async-start | bytes 524288 | tf_op jit(solution)/shard_map/all_to_all | solution.py:78
  25.8 25.1 %copy-start.3 = (s32[32,8]{0,1:T(8,128)S(1)}, s32[32,8]{0,1:T(8,128)}, u32[]{:S(2)}) copy-start(s32[32,8]{0,1:T(8,128)} %param.19) | copy-start | bytes 3076
  25.8 35.7 %copy-start.1 = (bf16[32,4096]{1,0:T(8,128)(2,1)S(1)}, bf16[32,4096]{1,0:T(8,128)(2,1)}, u32[]{:S(2)}) copy-start(bf16[32,4096]{1,0:T(8,128)(2,1)} %param.17) | copy-start | bytes 786436
  26.0 35.7 %copy-start.2 = (f32[4096]{0:T(1024)S(1)}, f32[4096]{0:T(1024)}, u32[]{:S(2)}) copy-start(f32[4096]{0:T(1024)} %param.18) | copy-start | bytes 49156
  48.3 13.2 %all-to-all-start.1 = ((bf16[32,32,128]{2,1,0:T(8,128)(2,1)}), bf16[32,32,128]{2,1,0:T(8,128)(2,1)S(1)}, u32[]{:S(2)}, u32[]{:S(2)}) async-start(bf16[32,32,128]{2,1,0:T(8,128)(2,1)} %constant_dynamic-update-slice_fusion), calls=%async_computation.1 | async-start | bytes 524288 | tf_op jit(solution)/shard_map/all_to_all | solution.py:64
  76.5 2.0 %collective-permute-start = (bf16[32,1,4096]{2,1,0:T(2,128)(2,1)S(1)}, bf16[32,1,4096]{2,1,0:T(2,128)(2,1)S(1)}, u32[]{:S(2)}, u32[]{:S(2)}) collective-permute-start(bf16[32,1,4096]{2,1,0:T(2,128)(2,1)S(1)} %reshape.172), channel_id=1, source_target_pairs={{0,1},{1,0},{2,3},{3,2},{4,5},{5,4},{6,7},{7,6},{8,9},{9,8},{10,11... | collective-permute-start | bytes 786440 | tf_op jit(solution)/shard_map/ppermute | solution.py:17
  80.8 14.0 %collective-permute-start.1 = (bf16[32,2,4096]{2,1,0:T(2,128)(2,1)S(1)}, bf16[32,2,4096]{2,1,0:T(2,128)(2,1)S(1)}, u32[]{:S(2)}, u32[]{:S(2)}) collective-permute-start(bf16[32,2,4096]{2,1,0:T(2,128)(2,1)S(1)} %broadcast_select_fusion), channel_id=1, source_target_pairs={{0,2},{1,3},{2,0},{3,1},{4,6},{5,7},{6,4},{7,5},{8,10},{9,11},{10,... | collective-permute-start | bytes 1572872 | tf_op jit(solution)/shard_map/ppermute | solution.py:17
  96.8 24.5 %collective-permute-start.2 = (bf16[32,4,4096]{2,1,0:T(4,128)(2,1)S(1)}, bf16[32,4,4096]{2,1,0:T(4,128)(2,1)}, u32[]{:S(2)}, u32[]{:S(2)}) collective-permute-start(bf16[32,4,4096]{2,1,0:T(4,128)(2,1)S(1)} %maximum_select_fusion.1), channel_id=1, source_target_pairs={{0,4},{1,5},{2,6},{3,7},{4,0},{5,1},{6,2},{7,3},{8,12},{9,13},{10,... | collective-permute-start | bytes 3145736 | tf_op jit(solution)/shard_map/ppermute | solution.py:17
  131.8 4.2 %copy-start.5 = (f32[32,8]{0,1:T(8,128)S(1)}, f32[32,8]{0,1:T(8,128)}, u32[]{:S(2)}) copy-start(f32[32,8]{0,1:T(8,128)} %param.20) | copy-start | bytes 3076
  131.8 52.7 %all-to-all-start.3 = ((bf16[32,8,4096]{2,1,0:T(8,128)(2,1)}), bf16[32,8,4096]{2,1,0:T(8,128)(2,1)}, u32[]{:S(2)}, u32[]{:S(2)}) async-start(bf16[32,8,4096]{2,1,0:T(8,128)(2,1)} %fusion.49), calls=%async_computation.3 | async-start | bytes 4194304 | tf_op jit(solution)/shard_map/all_to_all | solution.py:122
